TPU v7x, 32 devices: a whole 2x2x4 slice. The times are simulated.
32 devices in a mesh: dp: 4 (over y, x), blk: 8 (over z, core).
Axes of the slice: x: 2, y: 2, z: 4, core: 2. Of those that a mesh axis runs over, the one named last changes fastest.
Arguments:
- queries: bfloat16 [8192, 1664], P(('dp', 'blk')), parts along dimension 0, as said below
- keys: bfloat16 [8192, 1664], P(('dp', 'blk')), parts along dimension 0, as said below
- values: bfloat16 [8192, 1664], P(('dp', 'blk')), parts along dimension 0, may hold values from -6 to 6
- residual_in: bfloat16 [8192, 1664], P(('dp', 'blk')), parts along dimension 0, as said below
- out_proj: bfloat16 [1664, 1664], replicated, may hold values from -0.15625 to 0.15625
- ln_gain: float32 [1664], replicated, may hold values from 0.1 to 1.9
- merge_proj: bfloat16 [6656, 4096], P('blk'), as said below
- out_gain: float32 [4096], replicated, may hold values from 0.1 to 1.9
- image_rows: int32 [16], P('dp'), parts along dimension 0, may hold values from 1 to 192, 512 in all
- owners: int32 [2048, 1], P(('dp', 'blk')), parts along dimension 0, may hold values from 0 to 7; in each aligned block of 64 rows (0 to 63, 64 to 127, ...) at most 16 rows name the same one
Outputs:
- delivered: bfloat16 [4096, 4096], P(('dp', 'blk')), parts along dimension 0
There are 4 independent parts, one for each index of `dp`. A program takes and returns all parts, laid end to end along the dimension named above; an argument that names none is the same for every part. Nothing has to cross between parts.
Inputs may be any that keep to these rules, and one draw needn't show every extreme that they name: `image_rows`: images lie end to end; their merged rows sum to 512, and one image has exactly the most. `owners`: among the merged rows of one block no owner is named more than 16 times. `queries`: Real-valued; no structure is promised. `keys`: Real-valued; no structure is promised. `residual_in`: Real-valued; no structure is promised. `merge_proj`: Real-valued; no structure is promised.
All inputs are finite; a program needn't handle non-finite values.
Results may differ from a plain program's by a relative error of at most 0.017.
Values may be sent and summed in bfloat16 or wider, within the bound.
A program may use at most 128 MiB of HBM per device.

v0:
```python
import jax
import jax.numpy as jnp
from jax import lax
from jax.sharding import PartitionSpec as P

HEADS = 16


def passed_along(value, axis, steps):
    count = lax.axis_size(axis)
    first, last = (max(0, -steps), min(count, count - steps))
    return lax.ppermute(value, axis, [(source, source + steps) for source in range(first, last)])


def layer_norm(stream, gain):
    mean = jnp.mean(stream, axis=1, keepdims=True)
    centred = stream - mean
    var = jnp.mean(centred * centred, axis=1, keepdims=True)
    return centred * lax.rsqrt(var + 1e-06) * gain[None, :]


def on_device(
    queries, keys, values, residual_in, out_proj, ln_gain, merge_proj, out_gain, image_rows, owners
):
    blocks = lax.axis_size("blk")
    me_index = lax.axis_index("blk")
    tok, width = queries.shape
    row_count = tok // 4
    heads = HEADS
    hdim = width // heads
    reach = min(6, (blocks - 1) // 2)
    scale = 1.0 / hdim**0.5
    ends = jnp.cumsum(image_rows)

    def row_images(source):
        rows = source * row_count + jnp.arange(row_count, dtype=jnp.int32)
        found = jnp.sum((rows[:, None] >= ends[None, :]).astype(jnp.int32), axis=1)
        inside = jnp.logical_and(source >= 0, source < blocks)
        return jnp.where(inside, found, -1)

    def token_images(source):
        return jnp.repeat(row_images(source), 4, total_repeat_length=tok)

    query_img = token_images(me_index)
    q_heads = queries.reshape(tok, heads, hdim)
    own_pair = jnp.stack([keys, values])

    def masked_scores(pair, key_img):
        k_heads = pair[0].reshape(-1, heads, hdim)
        scores = (
            jnp.einsum("qhd,khd->hqk", q_heads, k_heads, preferred_element_type=jnp.float32) * scale
        )
        return jnp.where(query_img[None, :, None] == key_img[None, None, :], scores, -jnp.inf)

    def weigh_values(weights, pair):
        v_heads = pair[1].reshape(-1, heads, hdim)
        return jnp.einsum(
            "hqk,khd->hqd",
            weights.astype(jnp.bfloat16),
            v_heads,
            preferred_element_type=jnp.float32,
        )

    def absorb(state, pair, key_img):

        def update(carry):
            running_max, running_sum, accum = carry
            scores = masked_scores(pair, key_img)
            new_max = jnp.maximum(running_max, jnp.max(scores, axis=2, keepdims=True))
            factor = jnp.exp(running_max - new_max)
            weights = jnp.exp(scores - new_max)
            new_sum = running_sum * factor + jnp.sum(weights, axis=2, keepdims=True)
            new_accum = accum * factor + weigh_values(weights, pair)
            return (new_max, new_sum, new_accum)

        live = jnp.logical_and(
            jnp.max(key_img) >= jnp.maximum(jnp.min(query_img), 0),
            jnp.min(jnp.where(key_img >= 0, key_img, 1 << 30)) <= jnp.max(query_img),
        )
        return lax.cond(live, update, lambda carry: carry, state)

    first_scores = masked_scores(own_pair, query_img)
    first_max = jnp.max(first_scores, axis=2, keepdims=True)
    first_weights = jnp.exp(first_scores - first_max)
    state = (
        first_max,
        jnp.sum(first_weights, axis=2, keepdims=True),
        weigh_values(first_weights, own_pair),
    )
    from_left = own_pair
    from_right = own_pair
    for step in range(1, reach + 1):
        from_left = passed_along(from_left, "blk", 1)
        state = absorb(state, from_left, token_images(me_index - step))
        from_right = passed_along(from_right, "blk", -1)
        state = absorb(state, from_right, token_images(me_index + step))
    heads_out = state[2] / state[1]
    attended = heads_out.transpose(1, 0, 2).reshape(tok, width).astype(jnp.bfloat16)
    stream = residual_in.astype(jnp.float32) + jnp.dot(
        attended, out_proj, preferred_element_type=jnp.float32
    )
    normed = layer_norm(stream, ln_gain).astype(jnp.bfloat16)
    merged = normed.reshape(row_count, 4 * width)
    feature_rows = lax.all_to_all(merged, "blk", split_axis=1, concat_axis=0, tiled=True)
    projected = lax.psum_scatter(
        jnp.dot(feature_rows, merge_proj, preferred_element_type=jnp.float32).astype(jnp.bfloat16),
        "blk",
        scatter_dimension=0,
        tiled=True,
    ).astype(jnp.float32)
    my_rows_img = row_images(me_index)
    nimg = image_rows.shape[0]
    member = (my_rows_img[:, None] == jnp.arange(nimg, dtype=jnp.int32)[None, :]).astype(
        jnp.float32
    )
    row_squares = jnp.sum(projected * projected, axis=1)
    image_sums = lax.psum(jnp.sum(member * row_squares[:, None], axis=0), "blk")
    out_width = projected.shape[1]
    image_mean = image_sums / (image_rows.astype(jnp.float32) * out_width)
    row_scale = jnp.sum(member * lax.rsqrt(image_mean + 1e-06)[None, :], axis=1)
    scaled = (projected * row_scale[:, None] * out_gain[None, :]).astype(jnp.bfloat16)
    capacity = max(2, 2 * row_count // blocks)
    owner = owners[:, 0]
    onehot = (owner[:, None] == jnp.arange(blocks, dtype=jnp.int32)[None, :]).astype(jnp.int32)
    rank = jnp.sum(jnp.cumsum(onehot, axis=0) * onehot, axis=1) - 1
    slot = owner * capacity + rank
    placement = (jnp.arange(blocks * capacity, dtype=jnp.int32)[:, None] == slot[None, :]).astype(
        jnp.bfloat16
    )
    outgoing = jnp.dot(placement, scaled, preferred_element_type=jnp.float32).astype(jnp.bfloat16)
    return lax.all_to_all(outgoing, "blk", split_axis=0, concat_axis=0, tiled=True)


def solution(mesh):
    in_specs = (
        P(("dp", "blk"), None),
        P(("dp", "blk"), None),
        P(("dp", "blk"), None),
        P(("dp", "blk"), None),
        P(),
        P(),
        P("blk", None),
        P(),
        P("dp"),
        P(("dp", "blk"), None),
    )
    out_specs = P(("dp", "blk"), None)
    return jax.shard_map(
        on_device, mesh=mesh, in_specs=in_specs, out_specs=out_specs, check_vma=False
    )
```

profile of v0, /device:TPU:0, one launch (start us, length us, event | category | flops | bytes accessed | tf_op | source)
XLA Modules:
  0.0 259.8 jit_solution(6886633523841095833)
XLA Ops:
  6.5 0.0 reduce-scatter.2.cloned.1.call-start
  6.5 1.6 copy.43
  8.1 1.5 copy.44
  9.7 1.3 pad_maximum_fusion
  11.0 3.6 %collective-permute-start = (bf16[2,256,1664]{1,2,0:T(8,128)(2,1)}, bf16[2,256,1664]{1,2,0:T(8,128)(2,1)}, u32[]{:S(2)}, u32[]{:S(2)}) collective-permute-start(bf16[2,256,1664]{1,2,0:T(8,128)(2,1)} %pad_maximum_fusion), channel_id=1, source_target_pairs={{0,1},{1,2},{2,3},{3,4},{4,5},{5,6},{6,7},{8,9},{9,10},{10,11},{11... | collective-permute-start | bytes 5111816 | tf_op jit(solution)/shard_map/ppermute | solution.py:12
  14.6 1.3 collective-permute-start.1
  15.9 0.9 collective-permute-done
  16.9 21.3 %collective-permute-start.2 = (bf16[2,256,1664]{1,2,0:T(8,128)(2,1)}, bf16[2,256,1664]{1,2,0:T(8,128)(2,1)}, u32[]{:S(2)}, u32[]{:S(2)}) collective-permute-start(bf16[2,256,1664]{1,2,0:T(8,128)(2,1)} %collective-permute-done), channel_id=1, source_target_pairs={{0,1},{1,2},{2,3},{3,4},{4,5},{5,6},{6,7},{8,9},{9,10},{10,11},{11... | collective-permute-start | bytes 5111816 | tf_op jit(solution)/shard_map/ppermute | solution.py:12
  38.2 0.0 collective-permute-done.1
  38.2 1.3 collective-permute-start.3
  39.5 0.0 copy-done.7
  39.5 0.2 reduce-window.12
  39.7 0.0 copy-done.6
  39.7 0.1 compare_select_fusion
  39.8 0.1 convert_reduce_fusion
  39.9 1.9 gather_fusion.6
  41.8 0.7 fusion.107
  42.5 0.0 collective-permute-done.2
  42.5 19.1 %collective-permute-start.4 = (bf16[2,256,1664]{1,2,0:T(8,128)(2,1)}, bf16[2,256,1664]{1,2,0:T(8,128)(2,1)}, u32[]{:S(2)}, u32[]{:S(2)}) collective-permute-start(bf16[2,256,1664]{1,2,0:T(8,128)(2,1)} %collective-permute-done.2), channel_id=1, source_target_pairs={{0,1},{1,2},{2,3},{3,4},{4,5},{5,6},{6,7},{8,9},{9,10},{10,11},{11... | collective-permute-start | bytes 5111816 | tf_op jit(solution)/shard_map/ppermute | solution.py:12
  61.6 0.0 collective-permute-done.3
  61.6 1.3 collective-permute-start.5
  62.9 0.0 copy-done
  62.9 0.0 copy-start.1
  63.0 1.9 gather_fusion.5
  64.8 1.9 gather_fusion.4
  66.7 1.9 gather_fusion.3
  68.6 1.9 gather_fusion.2
  70.5 1.9 gather_fusion.1
  72.3 1.9 gather_fusion
  74.2 0.9 fusion.106
  87.2 0.0 copy-done.1
  87.2 0.6 copy.42
  87.8 0.1 broadcast_compare_fusion.6
  87.9 0.9 fusion.85
  88.8 0.9 fusion.87
  89.7 1.1 fusion.88
  90.7 0.2 conditional.7
  91.0 0.0 collective-permute-done.4
  91.0 0.2 conditional.10
  91.2 0.0 collective-permute-done.5
  91.2 0.0 copy-start.2
  91.3 0.2 divide_convert_fusion
  91.5 0.9 copy-done.2
  92.4 4.6 %fusion.117 = (f32[256]{0:T(256)S(1)}, f32[256,1664]{1,0:T(8,128)S(1)}) fusion(bf16[256,1664]{0,1:T(8,128)(2,1)S(1)} %bitcast.126, bf16[1664,1664]{1,0:T(8,128)(2,1)} %param.42, bf16[256,1664]{1,0:T(8,128)(2,1)S(1)} %copy-done.2), kind=kOutput, calls=%fused_computation.207 | convolution fusion | flops 1418952448 | bytes 8946688 | tf_op jit(solution)/shard_map/dot_general | solution.py:99
  96.9 0.3 multiply_reduce_fusion
  97.3 0.0 copy-done.4
  97.3 0.3 multiply_convert_fusion
  97.6 0.6 all_to_all.22
  98.2 0.1 copy.48
  98.3 42.5 %all_to_all.31 = bf16[64,8,832]{2,0,1:T(8,128)(2,1)S(1)} all-to-all(bf16[64,8,832]{2,0,1:T(8,128)(2,1)S(1)} %copy.48), channel_id=1, replica_groups=mesh['dp'=4,'blk'=8] {'blk'}, dimensions={1} | all-to-all | bytes 1703936 | tf_op jit(solution)/shard_map/all_to_all | solution.py:104
  140.8 9.1 %convolution_convert_fusion = bf16[512,4096]{1,0:T(8,128)(2,1)} fusion(bf16[512,832]{1,0:T(8,128)(2,1)S(1)} %bitcast.146, bf16[832,4096]{1,0:T(8,128)(2,1)} %param.44), kind=kOutput, calls=%fused_computation.116 | convolution fusion | flops 3491758080 | bytes 11862016 | tf_op jit(solution)/shard_map/dot_general | solution.py:106
  149.9 0.0 reduce-scatter.2.cloned.1.call-update
  149.9 0.6 copy-done.5
  150.6 0.1 fusion.101
  150.6 0.1 reduce_window_sum.59
  150.7 0.2 select_reduce_fusion
  150.9 55.3 %reduce-scatter.2.cloned.1.call-done = bf16[64,4096]{1,0:T(8,128)(2,1)} async-done(((bf16[512,4096]{1,0:T(8,128)(2,1)}), bf16[64,4096]{1,0:T(8,128)(2,1)}) %reduce-scatter.2.cloned.1.call-update) | async-done | bytes 524304 | tf_op jit(solution)/shard_map/reduce_scatter | solution.py:105
  206.2 1.2 fusion.94
  207.4 0.1 select_reduce_fusion.2
  207.6 13.8 %psum.7 = f32[4]{0:T(128)S(1)} all-reduce(f32[4]{0:T(128)S(1)} %select_reduce_fusion.2), channel_id=1, replica_groups=mesh['dp'=4,'blk'=8] {'blk'}, use_global_device_ids=true, to_apply=%region_55.57 | all-reduce | flops 4 | bytes 32 | tf_op jit(solution)/shard_map/psum | solution.py:117
  221.4 0.1 select_reduce_fusion.1
  221.5 1.5 convolution_convert_fusion.1
  223.0 29.0 %all_to_all.32 = bf16[8,16,4096]{2,1,0:T(8,128)(2,1)S(1)} all-to-all(bf16[8,16,4096]{2,1,0:T(8,128)(2,1)S(1)} %bitcast.127), channel_id=1, replica_groups=mesh['dp'=4,'blk'=8] {'blk'}, dimensions={0} | all-to-all | bytes 2097152 | tf_op jit(solution)/shard_map/all_to_all | solution.py:131
  252.0 1.0 copy.91
  (28 shorter events, 0.2 us)
Async XLA Ops:
  6.5 33.2 %copy-start.6 = (s32[2,128]{1,0:T(2,128)S(1)}, s32[2,128]{1,0:T(2,128)}, u32[]{:S(2)}) copy-start(s32[2,128]{1,0:T(2,128)} %constant.238.clone.1) | copy-start | bytes 3076
  6.5 33.0 %copy-start.7 = (s32[4]{0:T(128)S(1)}, s32[4]{0:T(128)}, u32[]{:S(2)}) copy-start(s32[4]{0:T(128)} %param.46) | copy-start | bytes 52
  6.5 199.7 %reduce-scatter.2.cloned.1.call-start = ((), (), s32[]{:S(2)}) async-start(), calls=%async_computation.3 | async-start | bytes 4718592 | tf_op jit(solution)/shard_map/reduce_scatter | solution.py:105
  11.0 5.9 %collective-permute-start = (bf16[2,256,1664]{1,2,0:T(8,128)(2,1)}, bf16[2,256,1664]{1,2,0:T(8,128)(2,1)}, u32[]{:S(2)}, u32[]{:S(2)}) collective-permute-start(bf16[2,256,1664]{1,2,0:T(8,128)(2,1)} %pad_maximum_fusion), channel_id=1, source_target_pairs={{0,1},{1,2},{2,3},{3,4},{4,5},{5,6},{6,7},{8,9},{9,10},{10,11},{11... | collective-permute-start | bytes 5111816 | tf_op jit(solution)/shard_map/ppermute | solution.py:12
  14.6 23.6 %collective-permute-start.1 = (bf16[2,256,1664]{1,2,0:T(8,128)(2,1)}, bf16[2,256,1664]{1,2,0:T(8,128)(2,1)S(1)}, u32[]{:S(2)}, u32[]{:S(2)}) collective-permute-start(bf16[2,256,1664]{1,2,0:T(8,128)(2,1)} %pad_maximum_fusion), channel_id=1, source_target_pairs={{1,0},{2,1},{3,2},{4,3},{5,4},{6,5},{7,6},{9,8},{10,9},{11,10},{12... | collective-permute-start | bytes 5111816 | tf_op jit(solution)/shard_map/ppermute | solution.py:12
  16.9 25.7 %collective-permute-start.2 = (bf16[2,256,1664]{1,2,0:T(8,128)(2,1)}, bf16[2,256,1664]{1,2,0:T(8,128)(2,1)}, u32[]{:S(2)}, u32[]{:S(2)}) collective-permute-start(bf16[2,256,1664]{1,2,0:T(8,128)(2,1)} %collective-permute-done), channel_id=1, source_target_pairs={{0,1},{1,2},{2,3},{3,4},{4,5},{5,6},{6,7},{8,9},{9,10},{10,11},{11... | collective-permute-start | bytes 5111816 | tf_op jit(solution)/shard_map/ppermute | solution.py:12
  38.2 24.8 %copy-start = (bf16[2,256,1664]{1,2,0:T(8,128)(2,1)}, bf16[2,256,1664]{1,2,0:T(8,128)(2,1)S(1)}, u32[]{:S(2)}) copy-start(bf16[2,256,1664]{1,2,0:T(8,128)(2,1)S(1)} %collective-permute-done.1) | copy-start | bytes 5111812
  38.2 23.5 %collective-permute-start.3 = (bf16[2,256,1664]{1,2,0:T(8,128)(2,1)S(1)}, bf16[2,256,1664]{1,2,0:T(8,128)(2,1)}, u32[]{:S(2)}, u32[]{:S(2)}) collective-permute-start(bf16[2,256,1664]{1,2,0:T(8,128)(2,1)S(1)} %collective-permute-done.1), channel_id=1, source_target_pairs={{1,0},{2,1},{3,2},{4,3},{5,4},{6,5},{7,6},{9,8},{10,9},{11,10},{12... | collective-permute-start | bytes 5111816 | tf_op jit(solution)/shard_map/ppermute | solution.py:12
  42.5 48.4 %collective-permute-start.4 = (bf16[2,256,1664]{1,2,0:T(8,128)(2,1)}, bf16[2,256,1664]{1,2,0:T(8,128)(2,1)}, u32[]{:S(2)}, u32[]{:S(2)}) collective-permute-start(bf16[2,256,1664]{1,2,0:T(8,128)(2,1)} %collective-permute-done.2), channel_id=1, source_target_pairs={{0,1},{1,2},{2,3},{3,4},{4,5},{5,6},{6,7},{8,9},{9,10},{10,11},{11... | collective-permute-start | bytes 5111816 | tf_op jit(solution)/shard_map/ppermute | solution.py:12
  61.6 29.6 %collective-permute-start.5 = (bf16[2,256,1664]{1,2,0:T(8,128)(2,1)}, bf16[2,256,1664]{1,2,0:T(8,128)(2,1)}, u32[]{:S(2)}, u32[]{:S(2)}) collective-permute-start(bf16[2,256,1664]{1,2,0:T(8,128)(2,1)} %collective-permute-done.3), channel_id=1, source_target_pairs={{1,0},{2,1},{3,2},{4,3},{5,4},{6,5},{7,6},{9,8},{10,9},{11,10},{12... | collective-permute-start | bytes 5111816 | tf_op jit(solution)/shard_map/ppermute | solution.py:12
  62.9 24.2 %copy-start.1 = (bf16[256,1664]{1,0:T(8,128)(2,1)S(1)}, bf16[256,1664]{1,0:T(8,128)(2,1)}, u32[]{:S(2)}) copy-start(bf16[256,1664]{1,0:T(8,128)(2,1)} %param.38) | copy-start | bytes 2555908
  91.2 1.2 copy-start.2
  92.4 4.9 %copy-start.4 = (f32[1664]{0:T(1024)S(1)}, f32[1664]{0:T(1024)}, u32[]{:S(2)}) copy-start(f32[1664]{0:T(1024)} %param.43) | copy-start | bytes 19972
  149.9 0.7 copy-start.5
  149.9 71.6 %copy-start.3 = (f32[4096]{0:T(1024)S(1)}, f32[4096]{0:T(1024)}, u32[]{:S(2)}) copy-start(f32[4096]{0:T(1024)} %param.45) | copy-start | bytes 49156
Sparse Core Ops, SparseCore 0:
  150.0 56.1 reduce-scatter.1
where the time goes:
time: 262 us; the launch traced here: 260 us
  blocking collectives  85.3 us (33%)
  waiting for transfers between devices  56.3 us (21%)
  starting transfers between devices  47.8 us (18%)
  between operations  25.9 us (10%)
  local copies, waits for them, and re-layouts  20.1 us (8%)
  matrix products  17.1 us (7%)
  other arithmetic  6.92 us (3%)
    reduce_scatter x1, waiting for transfers between devices, on_device(): lax.psum_scatter(jnp.dot(feature_rows, merge_proj, preferred_element_type...  55.3 us
    ppermute x6, starting transfers between devices, passed_along(): lax.ppermute(value, axis, [(source, source + steps) for source in range(f...  47.8 us
    all_to_all x1, blocking collectives, on_device(): lax.all_to_all(merged, 'blk', split_axis=1, concat_axis=0, tiled=True)  42.5 us
    all_to_all x1, blocking collectives, on_device(): lax.all_to_all(outgoing, 'blk', split_axis=0, concat_axis=0, tiled=True)  29 us
    psum x1, blocking collectives, on_device(): image_sums = lax.psum(jnp.sum(member * row_squares[:, None], axis=0), 'blk')  13.8 us
    gather x7, local copies, waits for them, and re-layouts, token_images(): return jnp.repeat(row_images(source), 4, total_repeat_length=tok)  13.1 us
    dot_general x1, matrix products, on_device(): jnp.dot(feature_rows, merge_proj, preferred_element_type=jnp.float32)  9.05 us
    unnamed x20, local copies, waits for them, and re-layouts  6.26 us
  transfers between devices with their start and end apart: 7, of which 2 were waited for; matrix products, arithmetic and copies ran while one was open for 7% of the time, Pallas kernels for 0%

commit v1 on v0

--- a/solution.py
+++ b/solution.py
@@ -1,7 +1,14 @@
 import jax
 import jax.numpy as jnp
 from jax import lax
+from jax.experimental import pallas as pl
+from jax.experimental.pallas import tpu as pltpu
 from jax.sharding import PartitionSpec as P
+
+MESH = pl.DeviceIdType.MESH
+CHIPS = 4
+PARTS = 2
+LANES = 128
 
 HEADS = 16
 
@@ -17,6 +24,305 @@
     centred = stream - mean
     var = jnp.mean(centred * centred, axis=1, keepdims=True)
     return centred * lax.rsqrt(var + 1e-06) * gain[None, :]
+
+
+def tail_kernel(
+    feats_in,
+    weight_hbm,
+    member_ref,
+    slot_member,
+    place_ref,
+    gain_ref,
+    count_ref,
+    out_ref,
+    weight,
+    feats,
+    keep,
+    give,
+    taken,
+    moving,
+    from_left,
+    from_right,
+    packed,
+    landed,
+    slot_images,
+    sums,
+    weight_sem,
+    feat_sems,
+    slot_sems,
+    pair_sems,
+    line_sems,
+    deliver_sems,
+    sum_sems,
+):
+    blocks, rows, depth = feats_in.shape
+    parts, width = keep.shape[0], keep.shape[3]
+    cap = slot_member.shape[1]
+    me = lax.axis_index("blk")
+    chip, core = me // 2, lax.rem(me, 2)
+    sibling = me + 1 - 2 * core
+
+    def send(src, dst, sems, index, landing, target):
+        return pltpu.make_async_remote_copy(
+            src_ref=src,
+            dst_ref=dst,
+            send_sem=sems.at[(0,) + index],
+            recv_sem=sems.at[(1,) + landing],
+            device_id={"blk": target},
+            device_id_type=MESH,
+        )
+
+    weight_copy = pltpu.make_async_copy(weight_hbm, weight, weight_sem)
+    weight_copy.start()
+
+    barrier = pltpu.get_barrier_semaphore()
+    others = [lax.rem(me + step, blocks) for step in (4, 5, 3, 6, 2, 7, 1)]
+    for other in others:
+        pl.semaphore_signal(barrier, inc=1, device_id={"blk": other}, device_id_type=MESH)
+    pl.semaphore_wait(barrier, blocks - 1)
+
+    for other in others:
+        send(feats_in.at[other], feats.at[me], feat_sems, (other,), (me,), other).start()
+    feats[me] = feats_in[me]
+    for other in others:
+        send(slot_member.at[other], slot_images.at[me], slot_sems, (other,), (me,), other).start()
+    slot_images[me] = slot_member[me]
+    weight_copy.wait()
+
+    def place_in_order(step):
+        far = jnp.maximum(chip, CHIPS - 1 - chip)
+        swapped = jnp.where(far == CHIPS - 1, step, 2 * CHIPS - 3 - step)
+        low = jnp.where(step < 2, step, swapped)
+        return jnp.where(chip >= 2, low, CHIPS - 1 - low)
+
+    def wait_feats(source):
+        @pl.when(source != me)
+        def _():
+            send(feats_in.at[source], feats.at[source], feat_sems, (source,), (source,), source).wait_recv()
+
+    tile = 1024
+
+    def multiply(part, first):
+        def one(step, unused):
+            to = place_in_order(step)
+            if first:
+                wait_feats(2 * to)
+                wait_feats(2 * to + 1)
+            lhs = jnp.concatenate([feats[2 * to + 1 - core], feats[2 * to + core]], axis=0)
+            for at in range(0, width, tile):
+                product = jnp.dot(
+                    lhs,
+                    weight[:, pl.ds(part * width + at, tile)],
+                    preferred_element_type=jnp.float32,
+                ).astype(jnp.bfloat16)
+                give[part, to, :, pl.ds(at, tile)] = product[:rows]
+                keep[part, to, :, pl.ds(at, tile)] = product[rows:]
+            send(give.at[part, to], taken.at[part, to], pair_sems, (part, to), (part, to), sibling).start()
+            return unused
+
+        lax.fori_loop(0, CHIPS, one, 0)
+
+    def pair_sum(part, to):
+        send(give.at[part, to], taken.at[part, to], pair_sems, (part, to), (part, to), sibling).wait_recv()
+
+    def pass_on(part, to, arrivals, direction, edge, way):
+        pair_sum(part, to)
+
+        @pl.when(edge)
+        def _():
+            moving[part, to] = (
+                keep[part, to].astype(jnp.float32) + taken[part, to].astype(jnp.float32)
+            ).astype(jnp.bfloat16)
+
+        @pl.when(jnp.logical_not(edge))
+        def _():
+            line_copy(part, to, arrivals, way, direction).wait_recv()
+            moving[part, to] = (
+                keep[part, to].astype(jnp.float32)
+                + taken[part, to].astype(jnp.float32)
+                + arrivals[part, to].astype(jnp.float32)
+            ).astype(jnp.bfloat16)
+
+        line_copy(part, to, arrivals, way, direction).start()
+
+    def line_copy(part, to, arrivals, way, direction):
+        target = jnp.clip(me + direction, 0, blocks - 1)
+        return pltpu.make_async_remote_copy(
+            src_ref=moving.at[part, to],
+            dst_ref=arrivals.at[part, to],
+            send_sem=line_sems.at[0, part, to],
+            recv_sem=line_sems.at[way, part, to],
+            device_id={"blk": target},
+            device_id_type=MESH,
+        )
+
+    def line_step(part, distance):
+        @pl.when(chip + distance < CHIPS)
+        def _():
+            pass_on(part, chip + distance, from_left, 2, chip == 0, 1)
+
+        @pl.when(chip - distance >= 0)
+        def _():
+            pass_on(part, chip - distance, from_right, -2, chip == CHIPS - 1, 2)
+
+    def finish(part, squares):
+        pair_sum(part, chip)
+
+        @pl.when(chip > 0)
+        def _():
+            line_copy(part, chip, from_left, 1, 2).wait_recv()
+
+        @pl.when(chip == 0)
+        def _():
+            from_left[part, chip] = jnp.zeros((rows, width), jnp.bfloat16)
+
+        @pl.when(chip < CHIPS - 1)
+        def _():
+            line_copy(part, chip, from_right, 2, -2).wait_recv()
+
+        @pl.when(chip == CHIPS - 1)
+        def _():
+            from_right[part, chip] = jnp.zeros((rows, width), jnp.bfloat16)
+
+        step = 512
+        for at in range(0, width, step):
+            cols = pl.ds(at, step)
+            total = (
+                keep[part, chip, :, cols].astype(jnp.float32)
+                + taken[part, chip, :, cols].astype(jnp.float32)
+                + from_left[part, chip, :, cols].astype(jnp.float32)
+                + from_right[part, chip, :, cols].astype(jnp.float32)
+            )
+            squares = squares + jnp.sum(total * total, axis=1, keepdims=True)
+            slots = jnp.dot(
+                place_ref[...], total.astype(jnp.bfloat16), preferred_element_type=jnp.float32
+            ).astype(jnp.bfloat16)
+            for owner in range(blocks):
+                packed[part, owner, :, cols] = slots[owner * cap : (owner + 1) * cap]
+        for other in others:
+            send(packed.at[part, other], landed.at[part, me], deliver_sems, (part, other), (part, me), other).start()
+        landed[part, me] = packed[part, me]
+        return squares
+
+    multiply(0, True)
+    line_step(0, CHIPS - 1)
+    for part in range(1, parts):
+        multiply(part, False)
+    for distance in range(CHIPS - 2, 0, -1):
+        line_step(0, distance)
+    squares = jnp.zeros((rows, 1), jnp.float32)
+    for part in range(parts):
+        if part + 1 < parts:
+            for distance in range(CHIPS - 1, 0, -1):
+                line_step(part + 1, distance)
+        squares = finish(part, squares)
+
+    mine = jnp.sum(member_ref[...] * squares, axis=0, keepdims=True)
+    sums[me] = jnp.broadcast_to(mine, (8, LANES))
+    for other in others:
+        send(sums.at[me], sums.at[me], sum_sems, (other,), (me,), other).start()
+    for other in others:
+        send(sums.at[me], sums.at[other], sum_sems, (other,), (other,), other).wait_recv()
+    total = sums[0]
+    for source in range(1, blocks):
+        total = total + sums[source]
+    inverse = lax.rsqrt(total / count_ref[...] + 1e-06)[0:1]
+
+    for step in range(blocks):
+        source = me if step == 0 else others[blocks - 1 - step]
+        if step:
+            send(slot_member.at[source], slot_images.at[source], slot_sems, (source,), (source,), source).wait_recv()
+        row_scale = jnp.sum(slot_images[source] * inverse, axis=1, keepdims=True)
+        lines = pl.ds(pl.multiple_of(source * cap, cap), cap)
+        for part in range(parts):
+            if step:
+                send(
+                    packed.at[part, source], landed.at[part, source], deliver_sems, (part, source), (part, source), source
+                ).wait_recv()
+            out_ref[lines, pl.ds(part * width, width)] = (
+                landed[part, source].astype(jnp.float32)
+                * row_scale
+                * gain_ref[:, pl.ds(part * width, width)]
+            ).astype(jnp.bfloat16)
+
+    for other in others:
+        send(feats_in.at[other], feats.at[me], feat_sems, (other,), (me,), other).wait_send()
+        send(slot_member.at[other], slot_images.at[me], slot_sems, (other,), (me,), other).wait_send()
+        send(sums.at[me], sums.at[me], sum_sems, (other,), (me,), other).wait_send()
+        for part in range(parts):
+            send(packed.at[part, other], landed.at[part, me], deliver_sems, (part, other), (part, me), other).wait_send()
+    for part in range(parts):
+        for to in range(CHIPS):
+            send(give.at[part, to], taken.at[part, to], pair_sems, (part, to), (part, to), sibling).wait_send()
+
+            @pl.when(chip < to)
+            def _():
+                line_copy(part, to, from_left, 1, 2).wait_send()
+
+            @pl.when(chip > to)
+            def _():
+                line_copy(part, to, from_right, 2, -2).wait_send()
+
+
+def merged_tail(merged, merge_proj, out_gain, image_rows, owner, my_rows_img, blocks):
+    rows = merged.shape[0]
+    depth, out_width = merge_proj.shape
+    nimg = image_rows.shape[0]
+    cap = max(2, 2 * rows // blocks)
+    width = out_width // PARTS
+    feats_in = merged.reshape(rows, blocks, depth).transpose(1, 0, 2)
+    lanes = jnp.arange(LANES, dtype=jnp.int32)
+    member = (my_rows_img[:, None] == lanes[None, :]).astype(jnp.float32)
+    onehot = (owner[:, None] == jnp.arange(blocks, dtype=jnp.int32)[None, :]).astype(jnp.int32)
+    rank = jnp.sum(jnp.cumsum(onehot, axis=0) * onehot, axis=1) - 1
+    slot = owner * cap + rank
+    filled = jnp.arange(blocks * cap, dtype=jnp.int32)[:, None] == slot[None, :]
+    place = filled.astype(jnp.bfloat16)
+    slot_img = jnp.sum(jnp.where(filled, my_rows_img[None, :] + 1, 0), axis=1) - 1
+    slot_member = (slot_img[:, None] == lanes[None, :]).astype(jnp.float32)
+    slot_member = slot_member.reshape(blocks, cap, LANES)
+    counts = jnp.ones((LANES,), jnp.float32).at[:nimg].set(
+        image_rows.astype(jnp.float32) * out_width
+    )
+    counts = jnp.broadcast_to(counts[None, :], (8, LANES))
+    vmem = pl.BlockSpec(memory_space=pltpu.VMEM)
+    tiles = (PARTS, CHIPS, rows, width)
+    half = jnp.bfloat16
+    return pl.pallas_call(
+        tail_kernel,
+        out_shape=jax.ShapeDtypeStruct((blocks * cap, out_width), half),
+        in_specs=[vmem, pl.BlockSpec(memory_space=pl.ANY)] + [vmem] * 5,
+        out_specs=vmem,
+        scratch_shapes=[
+            pltpu.VMEM((depth, out_width), half),
+            pltpu.VMEM((blocks, rows, depth), half),
+            pltpu.VMEM(tiles, half),
+            pltpu.VMEM(tiles, half),
+            pltpu.VMEM(tiles, half),
+            pltpu.VMEM(tiles, half),
+            pltpu.VMEM(tiles, half),
+            pltpu.VMEM(tiles, half),
+            pltpu.VMEM((PARTS, blocks, cap, width), half),
+            pltpu.VMEM((PARTS, blocks, cap, width), half),
+            pltpu.VMEM((blocks, cap, LANES), jnp.float32),
+            pltpu.VMEM((blocks, 8, LANES), jnp.float32),
+            pltpu.SemaphoreType.DMA,
+            pltpu.SemaphoreType.DMA((2, blocks)),
+            pltpu.SemaphoreType.DMA((2, blocks)),
+            pltpu.SemaphoreType.DMA((2, PARTS, CHIPS)),
+            pltpu.SemaphoreType.DMA((3, PARTS, CHIPS)),
+            pltpu.SemaphoreType.DMA((2, PARTS, blocks)),
+            pltpu.SemaphoreType.DMA((2, blocks)),
+        ],
+        compiler_params=pltpu.CompilerParams(
+            collective_id=0, has_side_effects=True, vmem_limit_bytes=44 * 1024 * 1024
+        ),
+        cost_estimate=pl.CostEstimate(
+            flops=2 * rows * blocks * depth * out_width,
+            bytes_accessed=2 * depth * out_width,
+            transcendentals=0,
+        ),
+    )(feats_in, merge_proj, member, slot_member, place, out_gain[None, :], counts)
 
 
 def on_device(
@@ -32,14 +338,16 @@
     scale = 1.0 / hdim**0.5
     ends = jnp.cumsum(image_rows)
 
-    def row_images(source):
-        rows = source * row_count + jnp.arange(row_count, dtype=jnp.int32)
+    def images_of(source, rows):
         found = jnp.sum((rows[:, None] >= ends[None, :]).astype(jnp.int32), axis=1)
         inside = jnp.logical_and(source >= 0, source < blocks)
         return jnp.where(inside, found, -1)
 
+    def row_images(source):
+        return images_of(source, source * row_count + jnp.arange(row_count, dtype=jnp.int32))
+
     def token_images(source):
-        return jnp.repeat(row_images(source), 4, total_repeat_length=tok)
+        return images_of(source, source * row_count + jnp.arange(tok, dtype=jnp.int32) // 4)
 
     query_img = token_images(me_index)
     q_heads = queries.reshape(tok, heads, hdim)
@@ -101,6 +409,10 @@
     )
     normed = layer_norm(stream, ln_gain).astype(jnp.bfloat16)
     merged = normed.reshape(row_count, 4 * width)
+    if blocks == 2 * CHIPS:
+        return merged_tail(
+            merged, merge_proj, out_gain, image_rows, owners[:, 0], row_images(me_index), blocks
+        )
     feature_rows = lax.all_to_all(merged, "blk", split_axis=1, concat_axis=0, tiled=True)
     projected = lax.psum_scatter(
         jnp.dot(feature_rows, merge_proj, preferred_element_type=jnp.float32).astype(jnp.bfloat16),

time: 262 us -> 185 us (0.71); the launches traced: 260 us -> 186 us
  Pallas kernels: 0 us -> 100 us
  blocking collectives: 85.3 us -> 0 us
  waiting for transfers between devices: 56.3 us -> 0.02 us
  starting transfers between devices: 47.8 us -> 28.3 us
  between operations: 25.9 us -> 12.8 us
  other arithmetic: 6.92 us -> 17.2 us
  matrix products: 17.1 us -> 10.6 us
  local copies, waits for them, and re-layouts: 20.1 us -> 16 us
    pallas_call x0 -> x1, Pallas kernels: none -> 100 us  [merged_tail(): pl.pallas_call(tail_kernel, out_shape=jax.ShapeDtypeStruct((blocks * cap,...]
    all_to_all x2 -> x0, blocking collectives: 71.5 us -> none  [the longest x1 42.5 us: on_device(): lax.all_to_all(merged, 'blk', split_axis=1, concat_axis=0, tiled=True)]
    reduce_scatter x1 -> x0, waiting for transfers between devices: 55.3 us -> none  [on_device(): lax.psum_scatter(jnp.dot(feature_rows, merge_proj, preferred_element_type...]
    ppermute x6, starting transfers between devices: 47.8 us -> 28.3 us  [passed_along(): lax.ppermute(value, axis, [(source, source + steps) for source in range(f...]
    psum x1 -> x0, blocking collectives: 13.8 us -> none  [on_device(): image_sums = lax.psum(jnp.sum(member * row_squares[:, None], axis=0), 'blk')]
    gather x7 -> x0, local copies, waits for them, and re-layouts: 13.1 us -> none  [token_images(): return jnp.repeat(row_images(source), 4, total_repeat_length=tok)]
    dot_general x2 -> x0, matrix products: 10.6 us -> none  [the longest x1 9.05 us: on_device(): jnp.dot(feature_rows, merge_proj, preferred_element_type=jnp.float32)]
    reduce_min x2 -> x6, other arithmetic: 1.57 us -> 7.17 us  [absorb(): jnp.min(jnp.where(key_img >= 0, key_img, 1 << 30)) <= jnp.max(query_img)]
  transfers between devices with their start and end apart: 7 -> 6, of which waited for: 2 -> 0; matrix products, arithmetic and copies ran while one was open for 7% -> 14% of each run, Pallas kernels for 0% -> 0%
where the time goes in v1:
time: 185 us; the launch traced here: 186 us
  Pallas kernels  100 us (54%)
  starting transfers between devices  28.3 us (15%)
  other arithmetic  17.2 us (9%)
  local copies, waits for them, and re-layouts  16 us (9%)
  between operations  12.8 us (7%)
  matrix products  10.6 us (6%)
    pallas_call x1, Pallas kernels, merged_tail(): pl.pallas_call(tail_kernel, out_shape=jax.ShapeDtypeStruct((blocks * cap,...  100 us
    ppermute x6, starting transfers between devices, passed_along(): lax.ppermute(value, axis, [(source, source + steps) for source in range(f...  28.3 us
    unnamed x38, local copies, waits for them, and re-layouts  8.92 us
    reduce_min x6, other arithmetic, absorb(): jnp.min(jnp.where(key_img >= 0, key_img, 1 << 30)) <= jnp.max(query_img)  7.17 us
    dot_general x1, matrix products, on_device(): jnp.dot(attended, out_proj, preferred_element_type=jnp.float32)  4.51 us
  transfers between devices with their start and end apart: 6, of which 0 were waited for; matrix products, arithmetic and copies ran while one was open for 14% of the time, Pallas kernels for 0%

profile of v1, /device:TPU:0, one launch (start us, length us, event | category | flops | bytes accessed | tf_op | source)
XLA Modules:
  0.0 185.8 jit_solution(2487468186949033433)
XLA Ops:
  0.0 1.6 copy.43
  1.6 1.5 copy.44
  3.2 1.4 pad_maximum_fusion
  4.5 3.5 %collective-permute-start = (bf16[2,256,1664]{1,2,0:T(8,128)(2,1)}, bf16[2,256,1664]{1,2,0:T(8,128)(2,1)}, u32[]{:S(2)}, u32[]{:S(2)}) collective-permute-start(bf16[2,256,1664]{1,2,0:T(8,128)(2,1)} %pad_maximum_fusion), channel_id=1, source_target_pairs={{0,1},{1,2},{2,3},{3,4},{4,5},{5,6},{6,7},{8,9},{9,10},{10,11},{11... | collective-permute-start | bytes 5111816 | tf_op jit(solution)/shard_map/ppermute | solution.py:19
  8.1 1.3 collective-permute-start.1
  9.4 0.2 reduce-window.8
  9.6 0.1 convert_reduce_fusion
  9.7 0.7 fusion.107
  11.1 1.3 fusion.98
  14.3 1.2 fusion.99
  17.5 1.2 fusion.100
  20.6 1.2 fusion.101
  23.7 1.2 fusion.102
  26.9 5.3 %collective-permute-start.2 = (bf16[2,256,1664]{1,2,0:T(8,128)(2,1)}, bf16[2,256,1664]{1,2,0:T(8,128)(2,1)}, u32[]{:S(2)}, u32[]{:S(2)}) collective-permute-start(bf16[2,256,1664]{1,2,0:T(8,128)(2,1)} %collective-permute-done), channel_id=1, source_target_pairs={{0,1},{1,2},{2,3},{3,4},{4,5},{5,6},{6,7},{8,9},{9,10},{10,11},{11... | collective-permute-start | bytes 5111816 | tf_op jit(solution)/shard_map/ppermute | solution.py:19
  32.2 1.3 collective-permute-start.3
  33.5 1.2 fusion.103
  36.6 0.6 copy.42
  37.2 0.1 fusion.96
  37.3 0.1 reduce_window_sum.18
  37.4 0.1 convert_reduce_fusion.7
  37.5 0.2 select_reduce_fusion.1
  37.6 0.6 broadcast_add_fusion.7
  38.2 0.1 select_reduce_fusion
  38.3 0.7 sub.153
  39.0 0.5 scatter.4
  39.5 0.1 broadcast_compare_fusion.6
  39.7 15.6 %collective-permute-start.4 = (bf16[2,256,1664]{1,2,0:T(8,128)(2,1)}, bf16[2,256,1664]{1,2,0:T(8,128)(2,1)}, u32[]{:S(2)}, u32[]{:S(2)}) collective-permute-start(bf16[2,256,1664]{1,2,0:T(8,128)(2,1)} %collective-permute-done.2), channel_id=1, source_target_pairs={{0,1},{1,2},{2,3},{3,4},{4,5},{5,6},{6,7},{8,9},{9,10},{10,11},{11... | collective-permute-start | bytes 5111816 | tf_op jit(solution)/shard_map/ppermute | solution.py:19
  55.2 1.3 collective-permute-start.5
  56.5 0.9 fusion.85
  57.4 1.5 fusion.87
  58.9 1.0 fusion.88
  60.0 0.1 fusion.97.member_ref
  60.1 0.1 fusion.95.slot_member
  60.2 0.6 copy-done.23
  60.8 5.5 %conditional.7 = ((f32[16,256,1]{1,0,2:T(8,128)S(1)}, f32[16,256,1]{1,0,2:T(8,128)}, f32[16,256,104]{1,2,0:T(8,128)S(1)})) conditional(s32[]{:T(128)} %convert_element_type.105, (f32[16,256,1]{1,0,2:T(8,128)S(1)}, f32[16,256,1]{1,0,2:T(8,128)}, f32[16,256,104]{1,2,0:T(8,128)S(1)}) %get-tuple-element.322, (s32[256]{0:T(256)}, s32[256]{0:T(256)S(1)}, ...), branch_computations={%region_28.29_spmd, %region_29.32_spmd} | conditional | flops 448671744 | bytes 22612056 | solution.py:388
  60.8 0.7 broadcast_compare_fusion.1
  61.5 1.5 fusion.110
  63.0 0.0 copy-start.4
  63.1 0.9 fusion.14
  64.0 0.9 fusion.16
  64.9 0.0 copy-start.5
  64.9 1.2 multiply_add_fusion.1
  66.3 0.6 copy-done.21
  66.9 5.3 %conditional.9 = ((f32[16,256,1]{1,0,2:T(8,128)S(1)}, f32[16,256,1]{1,0,2:T(8,128)}, f32[16,256,104]{1,2,0:T(8,128)S(1)})) conditional(s32[]{:T(128)} %convert_element_type.101, (f32[16,256,1]{1,0,2:T(8,128)S(1)}, f32[16,256,1]{1,0,2:T(8,128)}, f32[16,256,104]{1,2,0:T(8,128)S(1)}) %get-tuple-element.324, (s32[256]{0:T(256)}, s32[256]{0:T(256)S(1)}, ...), branch_computations={%region_36.37_spmd, %region_37.40_spmd} | conditional | flops 448671744 | bytes 22612056 | solution.py:388
  66.9 0.7 broadcast_compare_fusion.3
  67.7 1.5 fusion.112
  69.2 0.0 copy-start.8
  69.2 0.9 fusion.42
  70.1 0.9 fusion.44
  71.0 0.0 copy-start.9
  71.1 1.2 multiply_add_fusion.3
  72.3 0.0 copy-start.15
  72.3 0.2 conditional.11
  72.6 0.9 divide_convert_fusion
  73.5 0.0 copy-done.15
  73.5 4.5 %fusion.114 = (f32[256]{0:T(256)S(1)}, f32[256,1664]{1,0:T(8,128)S(1)}) fusion(bf16[256,1664]{0,1:T(8,128)(2,1)S(1)} %bitcast.123, bf16[1664,1664]{1,0:T(8,128)(2,1)} %param.28, bf16[256,1664]{1,0:T(8,128)(2,1)S(1)} %copy-done.15), kind=kOutput, calls=%fused_computation.191 | convolution fusion | flops 1418952448 | bytes 8946688 | tf_op jit(solution)/shard_map/dot_general | solution.py:407
  78.0 0.0 copy-start.1
  78.0 0.3 multiply_reduce_fusion
  78.4 0.3 multiply_convert_fusion
  78.7 1.5 reshape_reshape.3
  80.2 1.3 copy.57
  81.6 2.9 %copy-done = bf16[832,4096]{1,0:T(8,128)(2,1)S(1)} copy-done((bf16[832,4096]{1,0:T(8,128)(2,1)S(1)}, bf16[832,4096]{1,0:T(8,128)(2,1)}, u32[]{:S(2)}) %copy-start) | copy-done | bytes 6815768
  84.5 100.4 %shard_map.100 = bf16[128,4096]{1,0:T(8,128)(2,1)S(1)} custom-call(bf16[8,64,832]{2,1,0:T(8,128)(2,1)S(1)} %bitcast.110, bf16[832,4096]{1,0:T(8,128)(2,1)S(1)} %copy-done, f32[64,128]{1,0:T(8,128)S(1)} %fusion.97.member_ref, f32[8,16,128]{2,1,0:T(8,128)S(1)} %fusion.95.slot_member, bf16[128,64]{1,0:T(8,128)(2,1)S(1)} %fusion.94.place_ref, ...), custom_call_target="tpu_custom_call" | custom-call | flops 3489660928 | bytes 6815744 | tf_op jit(solution)/shard_map/pallas_call | solution.py:291
  184.9 1.0 copy.93
  (58 shorter events, 0.2 us)
Async XLA Ops:
  0.0 9.4 %copy-start.28 = (s32[4]{0:T(128)S(1)}, s32[4]{0:T(128)}, u32[]{:S(2)}) copy-start(s32[4]{0:T(128)} %param.32) | copy-start | bytes 52
  0.0 36.6 %copy-start.14 = (bf16[256,1664]{1,0:T(8,128)(2,1)S(1)}, bf16[256,1664]{1,0:T(8,128)(2,1)}, u32[]{:S(2)}) copy-start(bf16[256,1664]{1,0:T(8,128)(2,1)} %param.24) | copy-start | bytes 2555908
  0.0 37.2 %copy-start.19 = (s32[64,1]{0,1:T(1,128)S(1)}, s32[64,1]{0,1:T(1,128)}, u32[]{:S(2)}) copy-start(s32[64,1]{0,1:T(1,128)} %param.33) | copy-start | bytes 772
  4.5 22.3 %collective-permute-start = (bf16[2,256,1664]{1,2,0:T(8,128)(2,1)}, bf16[2,256,1664]{1,2,0:T(8,128)(2,1)}, u32[]{:S(2)}, u32[]{:S(2)}) collective-permute-start(bf16[2,256,1664]{1,2,0:T(8,128)(2,1)} %pad_maximum_fusion), channel_id=1, source_target_pairs={{0,1},{1,2},{2,3},{3,4},{4,5},{5,6},{6,7},{8,9},{9,10},{10,11},{11... | collective-permute-start | bytes 5111816 | tf_op jit(solution)/shard_map/ppermute | solution.py:19
  8.1 24.1 %collective-permute-start.1 = (bf16[2,256,1664]{1,2,0:T(8,128)(2,1)}, bf16[2,256,1664]{1,2,0:T(8,128)(2,1)}, u32[]{:S(2)}, u32[]{:S(2)}) collective-permute-start(bf16[2,256,1664]{1,2,0:T(8,128)(2,1)} %pad_maximum_fusion), channel_id=1, source_target_pairs={{1,0},{2,1},{3,2},{4,3},{5,4},{6,5},{7,6},{9,8},{10,9},{11,10},{12... | collective-permute-start | bytes 5111816 | tf_op jit(solution)/shard_map/ppermute | solution.py:19
  10.4 48.5 %copy-start.16 = (s32[256]{0:T(256)}, s32[256]{0:T(256)S(1)}, u32[]{:S(2)}) copy-start(s32[256]{0:T(256)S(1)} %get-tuple-element.249) | copy-start | bytes 3076
  26.9 12.8 %collective-permute-start.2 = (bf16[2,256,1664]{1,2,0:T(8,128)(2,1)}, bf16[2,256,1664]{1,2,0:T(8,128)(2,1)}, u32[]{:S(2)}, u32[]{:S(2)}) collective-permute-start(bf16[2,256,1664]{1,2,0:T(8,128)(2,1)} %collective-permute-done), channel_id=1, source_target_pairs={{0,1},{1,2},{2,3},{3,4},{4,5},{5,6},{6,7},{8,9},{9,10},{10,11},{11... | collective-permute-start | bytes 5111816 | tf_op jit(solution)/shard_map/ppermute | solution.py:19
  32.2 23.1 %collective-permute-start.3 = (bf16[2,256,1664]{1,2,0:T(8,128)(2,1)}, bf16[2,256,1664]{1,2,0:T(8,128)(2,1)}, u32[]{:S(2)}, u32[]{:S(2)}) collective-permute-start(bf16[2,256,1664]{1,2,0:T(8,128)(2,1)} %collective-permute-done.1), channel_id=1, source_target_pairs={{1,0},{2,1},{3,2},{4,3},{5,4},{6,5},{7,6},{9,8},{10,9},{11,10},{12... | collective-permute-start | bytes 5111816 | tf_op jit(solution)/shard_map/ppermute | solution.py:19
  38.2 20.7 %copy-start.25 = (s32[64]{0:T(128)}, s32[64]{0:T(128)S(1)}, u32[]{:S(2)}) copy-start(s32[64]{0:T(128)S(1)} %get-tuple-element.287) | copy-start | bytes 772
  39.7 32.6 %collective-permute-start.4 = (bf16[2,256,1664]{1,2,0:T(8,128)(2,1)}, bf16[2,256,1664]{1,2,0:T(8,128)(2,1)}, u32[]{:S(2)}, u32[]{:S(2)}) collective-permute-start(bf16[2,256,1664]{1,2,0:T(8,128)(2,1)} %collective-permute-done.2), channel_id=1, source_target_pairs={{0,1},{1,2},{2,3},{3,4},{4,5},{5,6},{6,7},{8,9},{9,10},{10,11},{11... | collective-permute-start | bytes 5111816 | tf_op jit(solution)/shard_map/ppermute | solution.py:19
  55.2 17.1 %collective-permute-start.5 = (bf16[2,256,1664]{1,2,0:T(8,128)(2,1)}, bf16[2,256,1664]{1,2,0:T(8,128)(2,1)}, u32[]{:S(2)}, u32[]{:S(2)}) collective-permute-start(bf16[2,256,1664]{1,2,0:T(8,128)(2,1)} %collective-permute-done.3), channel_id=1, source_target_pairs={{1,0},{2,1},{3,2},{4,3},{5,4},{6,5},{7,6},{9,8},{10,9},{11,10},{12... | collective-permute-start | bytes 5111816 | tf_op jit(solution)/shard_map/ppermute | solution.py:19
  58.9 1.1 copy-start.24
  58.9 1.2 copy-start.17
  58.9 1.0 copy-start.26
  60.2 0.6 copy-start.23
  60.8 5.5 %copy-start.22 = (s32[256]{0:T(256)S(1)}, s32[256]{0:T(256)}, u32[]{:S(2)}) copy-start(s32[256]{0:T(256)} %get-tuple-element.246) | copy-start | bytes 3076
  63.0 1.8 copy-start.4
  64.9 1.2 copy-start.5
  66.3 0.6 copy-start.21
  66.9 5.4 %copy-start.20 = (s32[256]{0:T(256)S(1)}, s32[256]{0:T(256)}, u32[]{:S(2)}) copy-start(s32[256]{0:T(256)} %get-tuple-element.248) | copy-start | bytes 3076
  69.2 1.8 copy-start.8
  71.0 1.2 copy-start.9
  72.3 1.2 copy-start.15
  73.5 4.9 %copy-start.18 = (f32[1664]{0:T(1024)S(1)}, f32[1664]{0:T(1024)}, u32[]{:S(2)}) copy-start(f32[1664]{0:T(1024)} %param.29) | copy-start | bytes 19972
  78.0 3.5 %copy-start.27 = (f32[128]{0:T(128)S(1)}, f32[128]{0:T(128)}, u32[]{:S(2)}) copy-start(f32[128]{0:T(128)} %scatter.4) | copy-start | bytes 1540
  78.0 3.5 %copy-start.1 = (f32[4096]{0:T(1024)S(1)}, f32[4096]{0:T(1024)}, u32[]{:S(2)}) copy-start(f32[4096]{0:T(1024)} %param.31) | copy-start | bytes 49156
  81.5 2.9 %copy-start = (bf16[832,4096]{1,0:T(8,128)(2,1)S(1)}, bf16[832,4096]{1,0:T(8,128)(2,1)}, u32[]{:S(2)}) copy-start(bf16[832,4096]{1,0:T(8,128)(2,1)} %weight_hbm.1) | copy-start | bytes 20447236
